TPU v7x, 768 devices: a whole 4x8x12 slice. The times are simulated.
768 devices in a mesh: pb: 96 (over x, z, core), pa: 8 (over y).
Axes of the slice: x: 4, y: 8, z: 12, core: 2. Of those that a mesh axis runs over, the one named last changes fastest.
Arguments:
- queries: bfloat16 [12288, 4096], P('pb'), may hold values from -0.09375 to 0.09375
- positives: bfloat16 [12288, 4096], P(('pb', 'pa')), may hold values from -0.09375 to 0.09375
- negative_pool: bfloat16 [768, 4096], P('pa'), may hold values from -0.09375 to 0.09375
- negatives: int32 [12288, 7], P('pb'), may hold values from 0 to 767
Outputs:
- query_grad: float32 [12288, 4096], P(('pb', 'pa'))
- positive_grad: float32 [12288, 4096], P(('pb', 'pa'))
- pool_grad: float32 [8, 96, 4096], P('pa', 'pb')
- losses: float32 [12288], P(('pb', 'pa'))
All inputs are finite; a program needn't handle non-finite values.
Results may differ from a plain program's by a relative error of at most 0.0065.
Values sent between devices are 32-bit elements; how exact they have to be, the bound alone decides.
A program may use at most 32 MiB of HBM per device.

v0:
```python
import jax
import jax.numpy as jnp
from jax import lax
from jax.sharding import PartitionSpec as P

SOFTMAX_TEMPER = 0.02
EPSILON = 1e-06


def unit_rows(values):
    widened = values.astype(jnp.float32)
    scales = lax.rsqrt(jnp.sum(widened * widened, axis=1) + EPSILON)
    return (widened, scales, (widened * scales[:, None]).astype(jnp.bfloat16))


def norm_back(widened, scales, upstream):
    inner = jnp.sum(widened * upstream, axis=1)
    cube = scales * scales * scales
    return scales[:, None] * upstream - (cube * inner)[:, None] * widened


def row_products(left, right):
    return lax.dot_general(
        left, right, (((1,), (1,)), ((), ())), preferred_element_type=jnp.float32
    )


def leading_product(left, right):
    return lax.dot_general(
        left, right, (((0,), (0,)), ((), ())), preferred_element_type=jnp.float32
    )


def on_device(queries, positives, negative_pool, negatives):
    share = positives.shape[0]
    block_rows = negative_pool.shape[0]
    block_index = lax.axis_index("pa")
    own_start = block_index * share
    query_wide, query_scale, normalized_queries = unit_rows(queries)
    passage_wide, passage_scale, normalized_passages = unit_rows(positives)
    bank_wide, bank_scale, normalized_bank_rows = unit_rows(negative_pool)
    batch_pair_scores = row_products(normalized_queries, normalized_passages) / SOFTMAX_TEMPER
    negative_bank_scores = row_products(normalized_queries, normalized_bank_rows) / SOFTMAX_TEMPER
    bank_ids = block_index * block_rows + lax.iota(jnp.int32, block_rows)
    counts = jnp.sum((negatives[:, :, None] == bank_ids[None, None, :]).astype(jnp.float32), axis=1)
    inbatch_exp = jnp.exp(batch_pair_scores)
    bank_exp = jnp.exp(negative_bank_scores) * counts
    local_totals = jnp.sum(inbatch_exp, axis=1) + jnp.sum(bank_exp, axis=1)
    partition_sums = lax.psum(local_totals, "pa")
    multiplier = 1.0 / (SOFTMAX_TEMPER * partition_sums)
    batch_pair_weight = (inbatch_exp * multiplier[:, None]).astype(jnp.bfloat16)
    negative_bank_weight = (bank_exp * multiplier[:, None]).astype(jnp.bfloat16)
    query_row_sum = lax.psum_scatter(
        jnp.dot(batch_pair_weight, normalized_passages, preferred_element_type=jnp.float32)
        + jnp.dot(negative_bank_weight, normalized_bank_rows, preferred_element_type=jnp.float32),
        "pa",
        scatter_dimension=0,
        tiled=True,
    )
    own_wide = lax.dynamic_slice_in_dim(query_wide, own_start, share, 0)
    own_scale = lax.dynamic_slice_in_dim(query_scale, own_start, share, 0)
    normalized_own_rows = lax.dynamic_slice_in_dim(normalized_queries, own_start, share, 0)
    query_incoming_gradient = (
        query_row_sum - normalized_passages.astype(jnp.float32) / SOFTMAX_TEMPER
    )
    query_grad = norm_back(own_wide, own_scale, query_incoming_gradient)
    passage_incoming_gradient = (
        leading_product(batch_pair_weight, normalized_queries)
        - normalized_own_rows.astype(jnp.float32) / SOFTMAX_TEMPER
    )
    positive_grad = norm_back(passage_wide, passage_scale, passage_incoming_gradient)
    own_scores = lax.dynamic_slice_in_dim(batch_pair_scores, own_start, share, 0)
    own_totals = lax.dynamic_slice_in_dim(partition_sums, own_start, share, 0)
    losses = jnp.log(own_totals) - jnp.diagonal(own_scores)
    slice_rows = block_rows // lax.axis_size("pb")
    bank_sum = lax.psum_scatter(
        leading_product(negative_bank_weight, normalized_queries),
        "pb",
        scatter_dimension=0,
        tiled=True,
    )
    slice_start = lax.axis_index("pb") * slice_rows
    slice_wide = lax.dynamic_slice_in_dim(bank_wide, slice_start, slice_rows, 0)
    slice_scale = lax.dynamic_slice_in_dim(bank_scale, slice_start, slice_rows, 0)
    pool_grad = norm_back(slice_wide, slice_scale, bank_sum)[None, :, :]
    return (query_grad, positive_grad, pool_grad, losses)


def solution(mesh):
    placed = (P("pb", None), P(("pb", "pa"), None), P("pa", None), P("pb", None))
    return jax.shard_map(
        on_device,
        mesh=mesh,
        in_specs=placed,
        out_specs=(
            P(("pb", "pa"), None),
            P(("pb", "pa"), None),
            P("pa", "pb", None),
            P(("pb", "pa")),
        ),
        check_vma=False,
    )
```

profile of v0, /device:TPU:1, one launch (start us, length us, event | category | flops | bytes accessed | tf_op | source)
XLA Modules:
  0.0 333.9 jit_solution(11852710057856152256)
XLA Ops:
  8.1 1.6 multiply_reduce_fusion
  9.7 0.3 multiply_convert_fusion
  10.0 0.1 fusion.2
  10.2 0.3 multiply_reduce_fusion.1
  10.5 0.4 exponential_reduce_fusion
  10.9 0.1 convert_reduce_fusion
  11.0 0.5 fusion.12
  11.6 14.7 %psum.7 = f32[128]{0:T(128)S(1)} all-reduce(f32[128]{0:T(128)S(1)} %add.75), channel_id=1, replica_groups=mesh['pb'=96,'pa'=8] {'pa'}, use_global_device_ids=true, to_apply=%region_6.0 | all-reduce | flops 128 | bytes 1024 | tf_op jit(solution)/shard_map/psum | solution.py:49
  26.3 1.6 fusion.6
  27.9 0.5 fusion.7
  28.4 1.9 convolution_add_fusion
  30.3 1.5 convert_element_type.33
  31.8 1.4 convert_element_type.37
  33.2 0.6 dynamic_slice.24
  35.7 1.3 dynamic-slice
  37.0 0.1 constant_dynamic-slice_fusion
  37.0 0.7 gather_fusion
  37.7 0.6 log_subtract_fusion
  38.3 278.9 %all-reduce.3.cloned.1.call-done = f32[96,4096]{1,0:T(8,128)} async-done(((f32[96,4096]{1,0:T(8,128)}), f32[96,4096]{1,0:T(8,128)}) %all-reduce.3.cloned.1.call-update) | async-done | bytes 1572880
  317.2 2.3 multiply_reduce_fusion.3
  320.1 2.9 subtract_bitcast_fusion
  323.1 1.4 fusion.4
  324.5 0.1 fusion.8
  324.6 1.9 fusion.5
  (23 shorter events, 0.2 us)
Async XLA Ops:
  8.0 1.7 copy-start.1
  8.0 309.2 %all-reduce.3.cloned.1.call-start = ((), (), s32[]{:S(2)}) async-start(), calls=%async_computation.2 | async-start | bytes 3145728
  8.1 1.9 copy-start.2
  8.1 2.1 copy-start
  10.0 0.9 copy-start.4
  27.9 295.2 %reduce-scatter.2.cloned.1.call-start = ((), (), s32[]{:S(2)}) async-start(), calls=%async_computation.1 | async-start | bytes 2359296 | tf_op jit(solution)/shard_map/reduce_scatter | solution.py:53
  323.0 1.5 copy-start.3
Sparse Core Ops, SparseCore 0:
  28.0 289.1 all-reduce.2
Sparse Core Ops, SparseCore 1:
  31.5 50.9 reduce-scatter.1
where the time goes:
time: 334 us
  waiting for transfers between devices  279 us (84%)
  between operations  18.2 us (5%)
  blocking collectives  14.7 us (4%)
  other arithmetic  13.1 us (4%)
  matrix products  6.3 us (2%)
    unnamed x3, waiting for transfers between devices  279 us
    psum x1, blocking collectives, on_device(): partition_sums = lax.psum(local_totals, 'pa')  14.7 us
  transfers between devices with their start and end apart: 2, of which 1 were waited for; matrix products, arithmetic and copies ran while one was open for 4% of the time, Pallas kernels for 0%

commit v1 on v0

v1 whole, which is shorter than its diff:
```python
import functools

import jax
import jax.numpy as jnp
from jax import lax
from jax.experimental import pallas as pl
from jax.experimental.pallas import tpu as pltpu
from jax.sharding import PartitionSpec as P

TEMPER = 0.02
INVERSE = 1.0 / TEMPER
EPSILON = 1e-06
NY, NX, NZ, NC = 8, 4, 12, 2
D = 4096
ROWS = 128
SHARE = 16
BANK = 96
NEG = 7
PIECE = 1024
NQ = D // PIECE
SUB = PIECE // 128
HALF_ROWS = BANK // NC
CHUNK = HALF_ROWS // NX
F32 = jnp.float32
BF16 = jnp.bfloat16
MESH = pl.DeviceIdType.MESH


def nt(left, right):
    return lax.dot_general(left, right, (((1,), (1,)), ((), ())), preferred_element_type=F32)


def iota(shape, dimension):
    return lax.broadcasted_iota(jnp.int32, shape, dimension)


def kernel(
    q_hbm, p_hbm, b_hbm, neg_hbm,
    qg_hbm, pg_hbm, bg_hbm, loss_hbm,
    rows, neg, part, own_row, passage_up, out_q, out_p, out_b, out_loss,
    totals, total_part, y_recv, bank, c_recv, x_recv1, x_recv2, z_send, z_recv,
    load_sem, store_sem, t_send_sem, t_recv_sem, y_send_sem, y_recv_sem,
    c_send_sem, c_recv_sem, x1_send_sem, x1_recv_sem, x2_send_sem, x2_recv_sem,
    z_send_sem, z_recv_sem,
):
    pb, pa = lax.axis_index("pb"), lax.axis_index("pa")
    core, z, x = pb % NC, (pb // NC) % NZ, pb // (NC * NZ)

    def at_y(step):
        return (pb, (pa + step) % NY)

    def at_x(step):
        return ((((x + step) % NX) * NZ + z) * NC + core, pa)

    def at_z(step):
        return ((x * NZ + (z + step) % NZ) * NC + core, pa)

    other_core = ((x * NZ + z) * NC + (1 - core), pa)

    barrier = pltpu.get_barrier_semaphore()
    partners = [other_core] + [at_x(1), at_x(NX - 1)]
    partners += [at_y(step) for step in range(1, NY)] + [at_z(step) for step in range(1, NZ)]
    for partner in partners:
        pl.semaphore_signal(barrier, inc=1, device_id=partner, device_id_type=MESH)

    loads = [
        pltpu.make_async_copy(q_hbm, rows.at[0:ROWS], load_sem.at[0]),
        pltpu.make_async_copy(b_hbm, rows.at[ROWS:ROWS + BANK], load_sem.at[1]),
        pltpu.make_async_copy(p_hbm, rows.at[ROWS + BANK:ROWS + BANK + SHARE], load_sem.at[2]),
        pltpu.make_async_copy(neg_hbm, neg, load_sem.at[3]),
    ]
    for load in loads:
        load.start()
    rows[ROWS + BANK + SHARE:2 * ROWS, :] = jnp.zeros((ROWS - BANK - SHARE, D), BF16)
    for load in loads:
        load.wait()

    lane = iota((ROWS, ROWS), 1)
    sub = iota((ROWS, ROWS), 0)
    eye = lane == sub

    def pick(mask, values, axis):
        return jnp.sum(jnp.where(mask, values, 0.0), axis=axis, keepdims=True)

    gram = nt(rows[...], rows[...])
    gram_q, raw, gram_c = gram[:ROWS, :ROWS], gram[:ROWS, ROWS:], gram[ROWS:, ROWS:]
    q_scale_col = lax.rsqrt(pick(eye, gram_q, 1) + EPSILON)
    q_scale_row = lax.rsqrt(pick(eye, gram_q, 0) + EPSILON)
    c_scale_row = lax.rsqrt(pick(eye, gram_c, 0) + EPSILON)
    scores = raw * (q_scale_col * INVERSE) * c_scale_row
    ids = jnp.where(lane < BANK, lane + pa * BANK, -1)
    counts = jnp.where((lane >= BANK) & (lane < BANK + SHARE), 1.0, 0.0)
    for k in range(NEG):
        counts = counts + jnp.where(neg[:, k:k + 1] == ids, 1.0, 0.0)
    exps = jnp.exp(scores) * counts
    exps_t = jnp.transpose(exps)
    total_part[...] = jnp.broadcast_to(jnp.sum(exps_t, axis=0, keepdims=True), (8, ROWS))
    totals[pl.ds(pa, 1)] = total_part[...][None]

    pl.semaphore_wait(barrier, len(partners))

    t_copies = []
    for step in range(1, NY):
        copy = pltpu.make_async_remote_copy(
            src_ref=total_part, dst_ref=totals.at[pa],
            send_sem=t_send_sem.at[step], recv_sem=t_recv_sem.at[pa],
            device_id=at_y(step), device_id_type=MESH)
        copy.start()
        t_copies.append(copy)

    weight = (exps * c_scale_row).astype(BF16)

    def part_piece(piece):
        for block in range(PIECE // 256):
            cols = pl.ds(piece * PIECE + block * 256, 256)
            part[:, cols] = jnp.dot(weight, rows[ROWS:, cols], preferred_element_type=F32)

    def y_rows(step):
        return pl.ds(pl.multiple_of(((pa + step) % NY) * SHARE, SHARE), SHARE)

    def y_distance(m):
        return 4 - (m + 1) // 2

    def y_pieces(s, m):
        half = s if m % 2 == 0 else 1 - s
        return (2 * half, 2 * half + 1)

    y_copies = []

    def y_copy(s, m, j):
        sign = 1 if s == 0 else -1
        piece = y_pieces(s, m)[j]
        return pltpu.make_async_remote_copy(
            src_ref=part.at[y_rows((sign * y_distance(m)) % NY), pl.ds(piece * PIECE, PIECE)],
            dst_ref=y_recv.at[s, m, j],
            send_sem=y_send_sem.at[s, m, j], recv_sem=y_recv_sem.at[s, m, j],
            device_id=at_y(sign % NY), device_id_type=MESH)

    def y_send(s, m, j):
        copy = y_copy(s, m, j)
        copy.start()
        y_copies.append(copy)

    part_piece(0)
    y_send(0, 0, 0)
    part_piece(2)
    y_send(1, 0, 0)
    part_piece(1)
    y_send(0, 0, 1)
    part_piece(3)
    y_send(1, 0, 1)
    for j in range(2):
        for s in range(2):
            y_send(s, 1, j)

    def y_step(m, j):
        for s in range(2):
            y_copy(s, m, j).wait_recv()
            sign = 1 if s == 0 else -1
            dest = y_rows((sign * (y_distance(m) - 1)) % NY)
            cols = pl.ds(y_pieces(s, m)[j] * PIECE, PIECE)
            part[dest, cols] = part[dest, cols] + y_recv[s, m, j]
            y_send(s, m + 2, j)

    for step in range(1, NY):
        origin = (pa + step) % NY
        pltpu.make_async_remote_copy(
            src_ref=total_part, dst_ref=totals.at[origin],
            send_sem=t_send_sem.at[step], recv_sem=t_recv_sem.at[origin],
            device_id=at_y(step), device_id_type=MESH).wait_recv()
    total_row = jnp.sum(totals[...], axis=0)[0:1, :]
    weight_t = (exps_t * (q_scale_row * INVERSE / total_row)).astype(BF16)
    order = jnp.where(sub < BANK, (sub % HALF_ROWS) * NC + sub // HALF_ROWS, sub)
    weight_t = jnp.dot(jnp.where(lane == order, 1.0, 0.0).astype(BF16), weight_t,
                       preferred_element_type=F32).astype(BF16)

    c_copies, x_copies, z_copies = [], [], []

    def core_rows(which):
        return pl.ds(pl.multiple_of(which * (HALF_ROWS * SUB), HALF_ROWS * SUB), HALF_ROWS * SUB)

    for piece in range(NQ):
        for block in range(PIECE // 256):
            cols = pl.ds(piece * PIECE + block * 256, 256)
            product = jnp.dot(weight_t, rows[0:ROWS, cols], preferred_element_type=F32)
            passage_up[:, cols] = product[BANK:BANK + SHARE, :]
            for r in range(BANK // 8):
                for c in range(2):
                    bank[piece, pl.ds(r * 8 * SUB + block * 2 + c, 8, stride=SUB), :] = (
                        product[r * 8:r * 8 + 8, c * 128:c * 128 + 128])
        copy = pltpu.make_async_remote_copy(
            src_ref=bank.at[piece, core_rows(1 - core)], dst_ref=c_recv.at[piece],
            send_sem=c_send_sem.at[piece], recv_sem=c_recv_sem.at[piece],
            device_id=other_core, device_id_type=MESH)
        copy.start()
        c_copies.append(copy)

    def x_rows(step):
        start = core * (HALF_ROWS * SUB) + ((x + step) % NX) * (CHUNK * SUB)
        return pl.ds(pl.multiple_of(start, CHUNK * SUB), CHUNK * SUB)

    def x_copy(stage, piece, s):
        sign = 1 if s == 0 else -1
        recv = x_recv1.at[piece] if stage == 1 else x_recv2.at[piece, s]
        send_sem = x1_send_sem.at[piece] if stage == 1 else x2_send_sem.at[piece, s]
        recv_sem = x1_recv_sem.at[piece] if stage == 1 else x2_recv_sem.at[piece, s]
        return pltpu.make_async_remote_copy(
            src_ref=bank.at[piece, x_rows(2 if stage == 1 else sign % NX)], dst_ref=recv,
            send_sem=send_sem, recv_sem=recv_sem,
            device_id=at_x(sign % NX), device_id_type=MESH)

    def x_send(stage, piece, s):
        copy = x_copy(stage, piece, s)
        copy.start()
        x_copies.append(copy)

    def c_step(batch):
        for s in range(2):
            piece = 2 * batch + s
            c_copies[piece].wait_recv()
            own = core_rows(core)
            bank[piece, own, :] = bank[piece, own, :] + c_recv[piece]
            x_send(1, piece, s)
        for s in range(2):
            x_send(2, 2 * batch + 1 - s, s)

    def x1_step(batch):
        for s in range(2):
            piece = 2 * batch + s
            sign = 1 if s == 0 else -1
            x_copy(1, piece, s).wait_recv()
            dest = x_rows(sign % NX)
            bank[piece, dest, :] = bank[piece, dest, :] + x_recv1[piece]
            x_send(2, piece, s)

    def z_copy(batch, step):
        return pltpu.make_async_remote_copy(
            src_ref=z_send.at[batch, (z + step) % NZ], dst_ref=z_recv.at[batch, z],
            send_sem=z_send_sem.at[batch, step], recv_sem=z_recv_sem.at[batch, z],
            device_id=at_z(step), device_id_type=MESH)

    def x2_step(batch):
        for s in range(2):
            piece = 2 * batch + s
            for t in range(2):
                x_copy(2, piece, t).wait_recv()
            total = bank[piece, x_rows(0), :] + x_recv2[piece, 0] + x_recv2[piece, 1]
            z_send[batch, :, s * SUB:(s + 1) * SUB, :] = total.reshape(CHUNK, SUB, 128)
        for step in range(1, NZ):
            copy = z_copy(batch, step)
            copy.start()
            z_copies.append(copy)
        z_recv[batch, pl.ds(z, 1)] = z_send[batch, pl.ds(z, 1)]

    def z_step(batch):
        for step in range(1, NZ):
            origin = (z + step) % NZ
            pltpu.make_async_remote_copy(
                src_ref=z_send.at[batch, 0], dst_ref=z_recv.at[batch, origin],
                send_sem=z_send_sem.at[batch, step], recv_sem=z_recv_sem.at[batch, origin],
                device_id=at_z(step), device_id_type=MESH).wait_recv()
        return jnp.sum(z_recv[batch], axis=0)

    def norm_back(wide, scale, upstream):
        inner = jnp.sum(wide * upstream, axis=1, keepdims=True)
        return scale * upstream - (scale * scale * scale * inner) * wide

    own_lane, own_sub = iota((SHARE, ROWS), 1), iota((SHARE, ROWS), 0)
    own_query = own_lane == own_sub + pa * SHARE
    q_scale_own = pick(own_query, q_scale_row, 1)
    total_own = pick(own_query, total_row, 1)
    p_scale_own = pick(own_lane == own_sub + BANK, c_scale_row, 1)

    y_step(0, 0)
    y_step(0, 1)
    c_step(0)
    y_step(1, 0)
    c_step(1)
    x1_step(0)
    y_step(1, 1)
    x1_step(1)
    x2_step(0)
    y_step(2, 0)
    x2_step(1)

    own_q_rows = pl.ds(pl.multiple_of(pa * SHARE, SHARE), SHARE)
    own_q = rows[own_q_rows, :].astype(F32)
    own_p = rows[ROWS + BANK:ROWS + BANK + SHARE, :].astype(F32)
    passage_v = passage_up[...] - own_q * (q_scale_own * INVERSE)
    out_p[...] = norm_back(own_p, p_scale_own, passage_v)
    store_p = pltpu.make_async_copy(out_p, pg_hbm, store_sem.at[0])
    store_p.start()
    own_score = pick(lane == sub - pa * SHARE + BANK, scores, 1)
    score_row = pick(lane == sub - pa * SHARE, own_score, 0)
    total_head = pick(own_lane == own_sub, total_own, 0)
    loss = jnp.log(jnp.where(own_lane[0:1] < SHARE, total_head, 1.0)) - score_row
    out_loss[...] = jnp.broadcast_to(loss, (8, ROWS))
    store_loss = pltpu.make_async_copy(out_loss, loss_hbm, store_sem.at[1])
    store_loss.start()

    y_step(2, 1)

    one_hot = jnp.where(iota((SHARE, ROWS), 1) == pb, 1.0, 0.0).astype(BF16)
    for block in range(D // 256):
        row = jnp.dot(one_hot, rows[ROWS:, block * 256:block * 256 + 256], preferred_element_type=F32)
        for c in range(2):
            own_row[block * 2 + c:block * 2 + c + 1, :] = row[0:1, c * 128:c * 128 + 128]

    y_step(3, 0)
    y_step(3, 1)
    y_step(4, 0)
    y_step(4, 1)

    wide = own_row[...]
    bank_v = jnp.concatenate([z_step(0), z_step(1)], axis=0)

    def whole(values):
        return jnp.sum(jnp.sum(values, axis=0, keepdims=True), axis=1, keepdims=True)

    scale = lax.rsqrt(whole(wide * wide) + EPSILON)
    out_b[...] = scale * bank_v - (scale * scale * scale * whole(wide * bank_v)) * wide
    store_b = pltpu.make_async_copy(out_b, bg_hbm, store_sem.at[2])
    store_b.start()

    inverse_own = INVERSE / total_own
    own = y_rows(0)
    inner = jnp.zeros((SHARE, 1), F32)
    for m in (5, 6):
        for j in range(2):
            for s in range(2):
                y_copy(s, m, j).wait_recv()
    for piece in range(NQ):
        half, j = piece // 2, piece % 2
        cols = pl.ds(piece * PIECE, PIECE)
        arrived = y_recv[0, 6 if half == 0 else 5, j] + y_recv[1, 5 if half == 0 else 6, j]
        value = (part[own, cols] + arrived) * inverse_own
        value = value - own_p[:, piece * PIECE:(piece + 1) * PIECE] * (p_scale_own * INVERSE)
        out_q[:, cols] = value
        inner = inner + jnp.sum(value * own_q[:, piece * PIECE:(piece + 1) * PIECE], axis=1, keepdims=True)
    out_q[...] = q_scale_own * out_q[...] - (q_scale_own * q_scale_own * q_scale_own * inner) * own_q
    store_q = pltpu.make_async_copy(out_q, qg_hbm, store_sem.at[3])
    store_q.start()

    for copy in t_copies + y_copies + c_copies + x_copies + z_copies:
        copy.wait_send()
    for store in (store_p, store_loss, store_b, store_q):
        store.wait()


def on_device(queries, positives, negative_pool, negatives):
    anywhere = pl.BlockSpec(memory_space=pl.ANY)
    dma = pltpu.SemaphoreType.DMA
    query_grad, positive_grad, pool_grad, losses = pl.pallas_call(
        kernel,
        out_shape=(
            jax.ShapeDtypeStruct((SHARE, D), F32),
            jax.ShapeDtypeStruct((SHARE, D), F32),
            jax.ShapeDtypeStruct((D // 128, 128), F32),
            jax.ShapeDtypeStruct((8, ROWS), F32),
        ),
        in_specs=[anywhere] * 4,
        out_specs=(anywhere,) * 4,
        scratch_shapes=[
            pltpu.VMEM((2 * ROWS, D), BF16),
            pltpu.VMEM((ROWS, NEG), jnp.int32),
            pltpu.VMEM((ROWS, D), F32),
            pltpu.VMEM((D // 128, 128), F32),
            pltpu.VMEM((SHARE, D), F32),
            pltpu.VMEM((SHARE, D), F32),
            pltpu.VMEM((SHARE, D), F32),
            pltpu.VMEM((D // 128, 128), F32),
            pltpu.VMEM((8, ROWS), F32),
            pltpu.VMEM((NY, 8, ROWS), F32),
            pltpu.VMEM((8, ROWS), F32),
            pltpu.VMEM((2, 7, 2, SHARE, PIECE), F32),
            pltpu.VMEM((NQ, BANK * SUB, 128), F32),
            pltpu.VMEM((NQ, HALF_ROWS * SUB, 128), F32),
            pltpu.VMEM((NQ, CHUNK * SUB, 128), F32),
            pltpu.VMEM((NQ, 2, CHUNK * SUB, 128), F32),
            pltpu.VMEM((2, CHUNK, 2 * SUB, 128), F32),
            pltpu.VMEM((2, CHUNK, 2 * SUB, 128), F32),
            dma((4,)), dma((4,)), dma((NY,)), dma((NY,)),
            dma((2, 7, 2)), dma((2, 7, 2)),
            dma((NQ,)), dma((NQ,)), dma((NQ,)), dma((NQ,)),
            dma((NQ, 2)), dma((NQ, 2)), dma((2, NZ)), dma((2, NZ)),
        ],
        compiler_params=pltpu.CompilerParams(
            collective_id=0, has_side_effects=True, vmem_limit_bytes=40 * 1024 * 1024),
    )(queries, positives, negative_pool, negatives)
    return query_grad, positive_grad, pool_grad.reshape(1, 1, D), losses[0, :SHARE]


def solution(mesh):
    placed = (P("pb", None), P(("pb", "pa"), None), P("pa", None), P("pb", None))
    return jax.shard_map(
        on_device,
        mesh=mesh,
        in_specs=placed,
        out_specs=(
            P(("pb", "pa"), None),
            P(("pb", "pa"), None),
            P("pa", "pb", None),
            P(("pb", "pa")),
        ),
        check_vma=False,
    )
```

time: 334 us -> 53.3 us (0.16)
  waiting for transfers between devices: 279 us -> 0 us
  Pallas kernels: 0 us -> 45.8 us
  between operations: 18.2 us -> 0.65 us
  blocking collectives: 14.7 us -> 0 us
  other arithmetic: 13.1 us -> 0 us
  matrix products: 6.3 us -> 0 us
  local copies, waits for them, and re-layouts: 2.61 us -> 6.57 us
    unnamed x3 -> x0, waiting for transfers between devices: 279 us -> none
    pallas_call x0 -> x1, Pallas kernels: none -> 45.8 us  [on_device(): pl.pallas_call(kernel, out_shape=(jax.ShapeDtypeStruct((SHARE, D), F32),...]
    psum x1 -> x0, blocking collectives: 14.7 us -> none  [on_device(): partition_sums = lax.psum(local_totals, 'pa')]
    dot_general x6 -> x0, matrix products: 6.3 us -> none  [the longest x2 3 us: leading_product(): lax.dot_general(left, right, (((0,), (0,)), ((), ())), preferred_element_...]
    unnamed x11 -> x10, local copies, waits for them, and re-layouts: 1.3 us -> 6.06 us
    reduce_sum x5 -> x0, other arithmetic: 4.41 us -> none  [the longest x1 2.26 us: norm_back(): inner = jnp.sum(widened * upstream, axis=1)]
  transfers between devices with their start and end apart: 2 -> 0, of which waited for: 1 -> 0; matrix products, arithmetic and copies ran while one was open for 4% -> 0% of each run, Pallas kernels for 0% -> 0%
where the time goes in v1:
time: 53.3 us; the launch traced here: 53 us
  Pallas kernels  45.8 us (86%)
  local copies, waits for them, and re-layouts  6.57 us (12%)
  between operations  0.65 us (1%)
    pallas_call x1, Pallas kernels, on_device(): pl.pallas_call(kernel, out_shape=(jax.ShapeDtypeStruct((SHARE, D), F32),...  45.8 us
    unnamed x10, local copies, waits for them, and re-layouts  6.06 us

profile of v1, /device:TPU:1, one launch (start us, length us, event | category | flops | bytes accessed | tf_op | source)
XLA Modules:
  0.0 53.0 jit_solution(3501107933344004269)
XLA Ops:
  0.6 0.8 %copy.8.neg_hbm = s32[128,7]{1,0:T(8,128)S(1)} copy(s32[128,7]{0,1:T(8,128)} %param.7) | data formatting | bytes 7168 | tf_op args[3]
  1.4 0.0 copy-start
  1.4 1.2 %copy-done = bf16[128,4096]{1,0:T(8,128)(2,1)S(1)} copy-done((bf16[128,4096]{1,0:T(8,128)(2,1)S(1)}, bf16[128,4096]{1,0:T(8,128)(2,1)}, u32[]{:S(2)}) %copy-start) | copy-done | bytes 1048600
  2.6 0.0 copy-start.1
  2.7 1.1 %copy-done.1 = bf16[96,4096]{1,0:T(8,128)(2,1)S(1)} copy-done((bf16[96,4096]{1,0:T(8,128)(2,1)S(1)}, bf16[96,4096]{1,0:T(8,128)(2,1)}, u32[]{:S(2)}) %copy-start.1) | copy-done | bytes 786456
  3.8 0.0 copy-start.2
  3.8 0.9 %copy-done.2 = bf16[16,4096]{1,0:T(8,128)(2,1)S(1)} copy-done((bf16[16,4096]{1,0:T(8,128)(2,1)S(1)}, bf16[16,4096]{1,0:T(8,128)(2,1)}, u32[]{:S(2)}) %copy-start.2) | copy-done | bytes 131096
  4.7 45.8 %shard_map.75 = (f32[16,4096]{1,0:T(8,128)S(1)}, f32[16,4096]{1,0:T(8,128)S(1)}, f32[32,128]{1,0:T(8,128)S(1)}, f32[8,128]{1,0:T(8,128)S(1)}) custom-call(bf16[128,4096]{1,0:T(8,128)(2,1)S(1)} %copy-done, bf16[16,4096]{1,0:T(8,128)(2,1)S(1)} %copy-done.2, bf16[96,4096]{1,0:T(8,128)(2,1)S(1)} %copy-done.1, s32[128,7]{1,0:T(8,128)S(1)} %copy.8.neg_hbm), custom_call_target="tpu_custom_call" | custom-call | tf_op jit(solution)/shard_map/pallas_call | solution.py:353
  50.5 0.5 slice_bitcast_fusion
  51.0 0.7 %copy.12 = f32[16,4096]{1,0:T(8,128)} copy(f32[16,4096]{1,0:T(8,128)S(1)} %get-tuple-element.16) | data formatting | bytes 524288
  51.7 0.7 %copy.13 = f32[16,4096]{1,0:T(8,128)} copy(f32[16,4096]{1,0:T(8,128)S(1)} %get-tuple-element.17) | data formatting | bytes 524288
  52.4 0.6 %copy.14 = f32[1,1,4096]{2,1,0:T(1,128)} copy(f32[1,1,4096]{2,1,0:T(1,128)S(1)} %bitcast.3) | data formatting | bytes 32768
Async XLA Ops:
  1.4 1.2 %copy-start = (bf16[128,4096]{1,0:T(8,128)(2,1)S(1)}, bf16[128,4096]{1,0:T(8,128)(2,1)}, u32[]{:S(2)}) copy-start(bf16[128,4096]{1,0:T(8,128)(2,1)} %q_hbm.1) | copy-start | bytes 3145732
  2.6 1.1 %copy-start.1 = (bf16[96,4096]{1,0:T(8,128)(2,1)S(1)}, bf16[96,4096]{1,0:T(8,128)(2,1)}, u32[]{:S(2)}) copy-start(bf16[96,4096]{1,0:T(8,128)(2,1)} %b_hbm.1) | copy-start | bytes 2359300
  3.8 0.9 %copy-start.2 = (bf16[16,4096]{1,0:T(8,128)(2,1)S(1)}, bf16[16,4096]{1,0:T(8,128)(2,1)}, u32[]{:S(2)}) copy-start(bf16[16,4096]{1,0:T(8,128)(2,1)} %p_hbm.1) | copy-start | bytes 393220

commit v2 on v1

--- a/solution.py
+++ b/solution.py
@@ -17,8 +17,10 @@
 BANK = 96
 NEG = 7
 PIECE = 1024
-NQ = D // PIECE
-SUB = PIECE // 128
+THIN = 512
+NT = D // THIN
+NB = NT // 2
+SUB = THIN // 128
 HALF_ROWS = BANK // NC
 CHUNK = HALF_ROWS // NX
 F32 = jnp.float32
@@ -57,23 +59,24 @@
 
     other_core = ((x * NZ + z) * NC + (1 - core), pa)
 
+    loads = []
+    for half in range(2):
+        cols = slice(half * (D // 2), (half + 1) * (D // 2))
+        for i, (source, first, count) in enumerate(
+                ((q_hbm, 0, ROWS), (b_hbm, ROWS, BANK), (p_hbm, ROWS + BANK, SHARE))):
+            loads.append(pltpu.make_async_copy(
+                source.at[:, cols], rows.at[first:first + count, cols], load_sem.at[half, i]))
+    load_neg = pltpu.make_async_copy(neg_hbm, neg, load_sem.at[0, 3])
+    for load in loads:
+        load.start()
+    load_neg.start()
+
     barrier = pltpu.get_barrier_semaphore()
     partners = [other_core] + [at_x(1), at_x(NX - 1)]
     partners += [at_y(step) for step in range(1, NY)] + [at_z(step) for step in range(1, NZ)]
     for partner in partners:
         pl.semaphore_signal(barrier, inc=1, device_id=partner, device_id_type=MESH)
-
-    loads = [
-        pltpu.make_async_copy(q_hbm, rows.at[0:ROWS], load_sem.at[0]),
-        pltpu.make_async_copy(b_hbm, rows.at[ROWS:ROWS + BANK], load_sem.at[1]),
-        pltpu.make_async_copy(p_hbm, rows.at[ROWS + BANK:ROWS + BANK + SHARE], load_sem.at[2]),
-        pltpu.make_async_copy(neg_hbm, neg, load_sem.at[3]),
-    ]
-    for load in loads:
-        load.start()
     rows[ROWS + BANK + SHARE:2 * ROWS, :] = jnp.zeros((ROWS - BANK - SHARE, D), BF16)
-    for load in loads:
-        load.wait()
 
     lane = iota((ROWS, ROWS), 1)
     sub = iota((ROWS, ROWS), 0)
@@ -82,33 +85,37 @@
     def pick(mask, values, axis):
         return jnp.sum(jnp.where(mask, values, 0.0), axis=axis, keepdims=True)
 
-    gram = nt(rows[...], rows[...])
-    gram_q, raw, gram_c = gram[:ROWS, :ROWS], gram[:ROWS, ROWS:], gram[ROWS:, ROWS:]
-    q_scale_col = lax.rsqrt(pick(eye, gram_q, 1) + EPSILON)
+    gram_left, gram_c = 0.0, 0.0
+    for half in range(2):
+        for load in loads[3 * half:3 * half + 3]:
+            load.wait()
+        cols = slice(half * (D // 2), (half + 1) * (D // 2))
+        gram_left = gram_left + nt(rows[:, cols], rows[:ROWS, cols])
+        gram_c = gram_c + nt(rows[ROWS:, cols], rows[ROWS:, cols])
+    gram_q, raw = gram_left[:ROWS], gram_left[ROWS:]
+    load_neg.wait()
     q_scale_row = lax.rsqrt(pick(eye, gram_q, 0) + EPSILON)
+    c_scale_col = lax.rsqrt(pick(eye, gram_c, 1) + EPSILON)
     c_scale_row = lax.rsqrt(pick(eye, gram_c, 0) + EPSILON)
-    scores = raw * (q_scale_col * INVERSE) * c_scale_row
-    ids = jnp.where(lane < BANK, lane + pa * BANK, -1)
-    counts = jnp.where((lane >= BANK) & (lane < BANK + SHARE), 1.0, 0.0)
+    scores = raw * c_scale_col * (q_scale_row * INVERSE)
+    ids = jnp.where(sub < BANK, sub + pa * BANK, -1)
+    counts = jnp.where((sub >= BANK) & (sub < BANK + SHARE), 1.0, 0.0)
     for k in range(NEG):
-        counts = counts + jnp.where(neg[:, k:k + 1] == ids, 1.0, 0.0)
-    exps = jnp.exp(scores) * counts
-    exps_t = jnp.transpose(exps)
+        counts = counts + jnp.where(neg[k:k + 1, :] == ids, 1.0, 0.0)
+    exps_t = jnp.exp(scores) * counts
     total_part[...] = jnp.broadcast_to(jnp.sum(exps_t, axis=0, keepdims=True), (8, ROWS))
     totals[pl.ds(pa, 1)] = total_part[...][None]
 
     pl.semaphore_wait(barrier, len(partners))
 
-    t_copies = []
     for step in range(1, NY):
         copy = pltpu.make_async_remote_copy(
             src_ref=total_part, dst_ref=totals.at[pa],
-            send_sem=t_send_sem.at[step], recv_sem=t_recv_sem.at[pa],
+            send_sem=t_send_sem, recv_sem=t_recv_sem,
             device_id=at_y(step), device_id_type=MESH)
         copy.start()
-        t_copies.append(copy)
-
-    weight = (exps * c_scale_row).astype(BF16)
+
+    weight = jnp.transpose(exps_t * c_scale_col).astype(BF16)
 
     def part_piece(piece):
         for block in range(PIECE // 256):
@@ -162,26 +169,21 @@
             part[dest, cols] = part[dest, cols] + y_recv[s, m, j]
             y_send(s, m + 2, j)
 
-    for step in range(1, NY):
-        origin = (pa + step) % NY
-        pltpu.make_async_remote_copy(
-            src_ref=total_part, dst_ref=totals.at[origin],
-            send_sem=t_send_sem.at[step], recv_sem=t_recv_sem.at[origin],
-            device_id=at_y(step), device_id_type=MESH).wait_recv()
+    pltpu.make_async_copy(totals.at[1:NY], totals.at[1:NY], t_recv_sem).wait()
     total_row = jnp.sum(totals[...], axis=0)[0:1, :]
     weight_t = (exps_t * (q_scale_row * INVERSE / total_row)).astype(BF16)
     order = jnp.where(sub < BANK, (sub % HALF_ROWS) * NC + sub // HALF_ROWS, sub)
     weight_t = jnp.dot(jnp.where(lane == order, 1.0, 0.0).astype(BF16), weight_t,
                        preferred_element_type=F32).astype(BF16)
 
-    c_copies, x_copies, z_copies = [], [], []
+    c_copies, x_copies = [], []
 
     def core_rows(which):
         return pl.ds(pl.multiple_of(which * (HALF_ROWS * SUB), HALF_ROWS * SUB), HALF_ROWS * SUB)
 
-    for piece in range(NQ):
-        for block in range(PIECE // 256):
-            cols = pl.ds(piece * PIECE + block * 256, 256)
+    for piece in range(NT):
+        for block in range(THIN // 256):
+            cols = pl.ds(piece * THIN + block * 256, 256)
             product = jnp.dot(weight_t, rows[0:ROWS, cols], preferred_element_type=F32)
             passage_up[:, cols] = product[BANK:BANK + SHARE, :]
             for r in range(BANK // 8):
@@ -215,12 +217,14 @@
         x_copies.append(copy)
 
     def c_step(batch):
-        for s in range(2):
-            piece = 2 * batch + s
+        for piece in (2 * batch, 2 * batch + 1):
             c_copies[piece].wait_recv()
             own = core_rows(core)
             bank[piece, own, :] = bank[piece, own, :] + c_recv[piece]
-            x_send(1, piece, s)
+
+    def x_first(batch):
+        for s in range(2):
+            x_send(1, 2 * batch + s, s)
         for s in range(2):
             x_send(2, 2 * batch + 1 - s, s)
 
@@ -233,12 +237,6 @@
             bank[piece, dest, :] = bank[piece, dest, :] + x_recv1[piece]
             x_send(2, piece, s)
 
-    def z_copy(batch, step):
-        return pltpu.make_async_remote_copy(
-            src_ref=z_send.at[batch, (z + step) % NZ], dst_ref=z_recv.at[batch, z],
-            send_sem=z_send_sem.at[batch, step], recv_sem=z_recv_sem.at[batch, z],
-            device_id=at_z(step), device_id_type=MESH)
-
     def x2_step(batch):
         for s in range(2):
             piece = 2 * batch + s
@@ -247,18 +245,15 @@
             total = bank[piece, x_rows(0), :] + x_recv2[piece, 0] + x_recv2[piece, 1]
             z_send[batch, :, s * SUB:(s + 1) * SUB, :] = total.reshape(CHUNK, SUB, 128)
         for step in range(1, NZ):
-            copy = z_copy(batch, step)
-            copy.start()
-            z_copies.append(copy)
+            pltpu.make_async_remote_copy(
+                src_ref=z_send.at[batch, (z + step) % NZ], dst_ref=z_recv.at[batch, z],
+                send_sem=z_send_sem.at[batch], recv_sem=z_recv_sem.at[batch],
+                device_id=at_z(step), device_id_type=MESH).start()
         z_recv[batch, pl.ds(z, 1)] = z_send[batch, pl.ds(z, 1)]
 
     def z_step(batch):
-        for step in range(1, NZ):
-            origin = (z + step) % NZ
-            pltpu.make_async_remote_copy(
-                src_ref=z_send.at[batch, 0], dst_ref=z_recv.at[batch, origin],
-                send_sem=z_send_sem.at[batch, step], recv_sem=z_recv_sem.at[batch, origin],
-                device_id=at_z(step), device_id_type=MESH).wait_recv()
+        rest = z_recv.at[batch, 1:NZ]
+        pltpu.make_async_copy(rest, rest, z_recv_sem.at[batch]).wait()
         return jnp.sum(z_recv[batch], axis=0)
 
     def norm_back(wide, scale, upstream):
@@ -271,17 +266,27 @@
     total_own = pick(own_query, total_row, 1)
     p_scale_own = pick(own_lane == own_sub + BANK, c_scale_row, 1)
 
+    c_step(0)
+    x_first(0)
+    c_step(1)
+    x_first(1)
     y_step(0, 0)
+    c_step(2)
+    c_step(3)
+    x1_step(0)
+    x_first(2)
     y_step(0, 1)
-    c_step(0)
+    x1_step(1)
+    x_first(3)
+    x2_step(0)
     y_step(1, 0)
-    c_step(1)
-    x1_step(0)
+    x1_step(2)
+    x2_step(1)
     y_step(1, 1)
-    x1_step(1)
-    x2_step(0)
+    x1_step(3)
+    x2_step(2)
     y_step(2, 0)
-    x2_step(1)
+    x2_step(3)
 
     own_q_rows = pl.ds(pl.multiple_of(pa * SHARE, SHARE), SHARE)
     own_q = rows[own_q_rows, :].astype(F32)
@@ -290,11 +295,9 @@
     out_p[...] = norm_back(own_p, p_scale_own, passage_v)
     store_p = pltpu.make_async_copy(out_p, pg_hbm, store_sem.at[0])
     store_p.start()
-    own_score = pick(lane == sub - pa * SHARE + BANK, scores, 1)
-    score_row = pick(lane == sub - pa * SHARE, own_score, 0)
-    total_head = pick(own_lane == own_sub, total_own, 0)
-    loss = jnp.log(jnp.where(own_lane[0:1] < SHARE, total_head, 1.0)) - score_row
-    out_loss[...] = jnp.broadcast_to(loss, (8, ROWS))
+    own_score = pick(own_query, scores[BANK:BANK + SHARE, :], 1)
+    loss = pick(own_lane == own_sub, jnp.log(total_own) - own_score, 0)
+    out_loss[...] = loss[:, :SHARE]
     store_loss = pltpu.make_async_copy(out_loss, loss_hbm, store_sem.at[1])
     store_loss.start()
 
@@ -310,17 +313,6 @@
     y_step(3, 1)
     y_step(4, 0)
     y_step(4, 1)
-
-    wide = own_row[...]
-    bank_v = jnp.concatenate([z_step(0), z_step(1)], axis=0)
-
-    def whole(values):
-        return jnp.sum(jnp.sum(values, axis=0, keepdims=True), axis=1, keepdims=True)
-
-    scale = lax.rsqrt(whole(wide * wide) + EPSILON)
-    out_b[...] = scale * bank_v - (scale * scale * scale * whole(wide * bank_v)) * wide
-    store_b = pltpu.make_async_copy(out_b, bg_hbm, store_sem.at[2])
-    store_b.start()
 
     inverse_own = INVERSE / total_own
     own = y_rows(0)
@@ -329,7 +321,7 @@
         for j in range(2):
             for s in range(2):
                 y_copy(s, m, j).wait_recv()
-    for piece in range(NQ):
+    for piece in range(D // PIECE):
         half, j = piece // 2, piece % 2
         cols = pl.ds(piece * PIECE, PIECE)
         arrived = y_recv[0, 6 if half == 0 else 5, j] + y_recv[1, 5 if half == 0 else 6, j]
@@ -341,10 +333,33 @@
     store_q = pltpu.make_async_copy(out_q, qg_hbm, store_sem.at[3])
     store_q.start()
 
-    for copy in t_copies + y_copies + c_copies + x_copies + z_copies:
+    def whole(values):
+        return jnp.sum(jnp.sum(values, axis=0, keepdims=True), axis=1, keepdims=True)
+
+    wide = own_row[...]
+    scale = lax.rsqrt(whole(wide * wide) + EPSILON)
+    for copy in y_copies + c_copies + x_copies:
         copy.wait_send()
-    for store in (store_p, store_loss, store_b, store_q):
+    pltpu.make_async_copy(totals.at[1:NY], totals.at[1:NY], t_send_sem).wait()
+    for batch in range(NB):
+        rest = z_send.at[batch, 1:NZ]
+        pltpu.make_async_copy(rest, rest, z_send_sem.at[batch]).wait()
+    for store in (store_p, store_loss, store_q):
         store.wait()
+
+    bank_v = jnp.concatenate([z_step(batch) for batch in range(NB)], axis=0)
+    out_b[...] = scale * bank_v - (scale * scale * scale * whole(wide * bank_v)) * wide
+    store_b = pltpu.make_async_copy(out_b, bg_hbm, store_sem.at[2])
+    store_b.start()
+    store_b.wait()
+
+
+def hand_over(*refs):
+    copies = [pltpu.make_async_copy(refs[i], refs[4 + i], refs[8].at[i]) for i in range(4)]
+    for copy in copies:
+        copy.start()
+    for copy in copies:
+        copy.wait()
 
 
 def on_device(queries, positives, negative_pool, negatives):
@@ -356,38 +371,51 @@
             jax.ShapeDtypeStruct((SHARE, D), F32),
             jax.ShapeDtypeStruct((SHARE, D), F32),
             jax.ShapeDtypeStruct((D // 128, 128), F32),
-            jax.ShapeDtypeStruct((8, ROWS), F32),
+            jax.ShapeDtypeStruct((1, SHARE), F32),
         ),
         in_specs=[anywhere] * 4,
         out_specs=(anywhere,) * 4,
         scratch_shapes=[
             pltpu.VMEM((2 * ROWS, D), BF16),
-            pltpu.VMEM((ROWS, NEG), jnp.int32),
+            pltpu.VMEM((NEG, ROWS), jnp.int32),
             pltpu.VMEM((ROWS, D), F32),
             pltpu.VMEM((D // 128, 128), F32),
             pltpu.VMEM((SHARE, D), F32),
             pltpu.VMEM((SHARE, D), F32),
             pltpu.VMEM((SHARE, D), F32),
             pltpu.VMEM((D // 128, 128), F32),
-            pltpu.VMEM((8, ROWS), F32),
+            pltpu.VMEM((1, SHARE), F32),
             pltpu.VMEM((NY, 8, ROWS), F32),
             pltpu.VMEM((8, ROWS), F32),
             pltpu.VMEM((2, 7, 2, SHARE, PIECE), F32),
-            pltpu.VMEM((NQ, BANK * SUB, 128), F32),
-            pltpu.VMEM((NQ, HALF_ROWS * SUB, 128), F32),
-            pltpu.VMEM((NQ, CHUNK * SUB, 128), F32),
-            pltpu.VMEM((NQ, 2, CHUNK * SUB, 128), F32),
-            pltpu.VMEM((2, CHUNK, 2 * SUB, 128), F32),
-            pltpu.VMEM((2, CHUNK, 2 * SUB, 128), F32),
-            dma((4,)), dma((4,)), dma((NY,)), dma((NY,)),
+            pltpu.VMEM((NT, BANK * SUB, 128), F32),
+            pltpu.VMEM((NT, HALF_ROWS * SUB, 128), F32),
+            pltpu.VMEM((NT, CHUNK * SUB, 128), F32),
+            pltpu.VMEM((NT, 2, CHUNK * SUB, 128), F32),
+            pltpu.VMEM((NB, CHUNK, 2 * SUB, 128), F32),
+            pltpu.VMEM((NB, CHUNK, 2 * SUB, 128), F32),
+            dma((2, 4)), dma((4,)), dma, dma,
             dma((2, 7, 2)), dma((2, 7, 2)),
-            dma((NQ,)), dma((NQ,)), dma((NQ,)), dma((NQ,)),
-            dma((NQ, 2)), dma((NQ, 2)), dma((2, NZ)), dma((2, NZ)),
+            dma((NT,)), dma((NT,)), dma((NT,)), dma((NT,)),
+            dma((NT, 2)), dma((NT, 2)), dma((NB,)), dma((NB,)),
         ],
         compiler_params=pltpu.CompilerParams(
             collective_id=0, has_side_effects=True, vmem_limit_bytes=40 * 1024 * 1024),
-    )(queries, positives, negative_pool, negatives)
-    return query_grad, positive_grad, pool_grad.reshape(1, 1, D), losses[0, :SHARE]
+    )(*[pltpu.with_memory_space_constraint(t, pltpu.HBM) for t in (queries, positives, negative_pool, negatives.T)])
+    query_grad, positive_grad, pool_grad, losses = pl.pallas_call(
+        hand_over,
+        out_shape=(
+            jax.ShapeDtypeStruct((SHARE, D), F32),
+            jax.ShapeDtypeStruct((SHARE, D), F32),
+            jax.ShapeDtypeStruct((D // 128, 128), F32),
+            jax.ShapeDtypeStruct((1, SHARE), F32),
+        ),
+        in_specs=[anywhere] * 4,
+        out_specs=(anywhere,) * 4,
+        scratch_shapes=[dma((4,))],
+        compiler_params=pltpu.CompilerParams(vmem_limit_bytes=4 * 1024 * 1024),
+    )(query_grad, positive_grad, pool_grad, losses)
+    return query_grad, positive_grad, pool_grad.reshape(1, 1, D), losses.reshape(SHARE)
 
 
 def solution(mesh):

time: 53.3 us -> 48.4 us (0.908)
  the two profiles are of different devices: /device:TPU:1 before, /device:TPU:8 now
where the time goes in v2:
time: 48.4 us; the launch traced here: 48.2 us
  Pallas kernels  47.6 us (98%)
  between operations  0.64 us (1%)
    pallas_call x1, Pallas kernels, on_device(): pl.pallas_call(kernel, out_shape=(jax.ShapeDtypeStruct((SHARE, D), F32),...  46.7 us

profile of v2, /device:TPU:8, one launch (start us, length us, event | category | flops | bytes accessed | tf_op | source)
XLA Modules:
  0.0 48.2 jit_solution(14776388772308532859)
XLA Ops:
  0.6 46.7 %shard_map.75 = (f32[16,4096]{1,0:T(8,128)S(1)}, f32[16,4096]{1,0:T(8,128)S(1)}, f32[32,128]{1,0:T(8,128)S(1)}, f32[1,16]{1,0:T(1,128)S(1)}) custom-call(bf16[128,4096]{1,0:T(8,128)(2,1)} %q_hbm.1, bf16[16,4096]{1,0:T(8,128)(2,1)} %p_hbm.1, bf16[96,4096]{1,0:T(8,128)(2,1)} %b_hbm.1, s32[7,128]{1,0:T(8,128)} %bitcast.3), custom_call_target="tpu_custom_call" | custom-call | tf_op jit(solution)/shard_map/pallas_call | solution.py:368
  47.4 0.8 %shard_map.76 = (f32[16,4096]{1,0:T(8,128)}, f32[16,4096]{1,0:T(8,128)}, f32[32,128]{1,0:T(8,128)}, f32[1,16]{1,0:T(1,128)}) custom-call(f32[16,4096]{1,0:T(8,128)S(1)} %get-tuple-element.12.refs_0_, f32[16,4096]{1,0:T(8,128)S(1)} %get-tuple-element.13.refs_1_, f32[32,128]{1,0:T(8,128)S(1)} %get-tuple-element.14.refs_2_, f32[1,16]{1,0:T(1,128)S(1)} %get-tuple-element.15.refs_3_), custom_call_target="tpu_custom_call" | custom-call | tf_op jit(solution)/shard_map/pallas_call | solution.py:405

commit v3 on v2

--- a/solution.py
+++ b/solution.py
@@ -19,6 +19,7 @@
 PIECE = 1024
 THIN = 512
 NT = D // THIN
+HUB = 9
 NB = NT // 2
 SUB = THIN // 128
 HALF_ROWS = BANK // NC
@@ -43,7 +44,7 @@
     totals, total_part, y_recv, bank, c_recv, x_recv1, x_recv2, z_send, z_recv,
     load_sem, store_sem, t_send_sem, t_recv_sem, y_send_sem, y_recv_sem,
     c_send_sem, c_recv_sem, x1_send_sem, x1_recv_sem, x2_send_sem, x2_recv_sem,
-    z_send_sem, z_recv_sem,
+    z_send_sem, z_recv_sem, all_here,
 ):
     pb, pa = lax.axis_index("pb"), lax.axis_index("pa")
     core, z, x = pb % NC, (pb // NC) % NZ, pb // (NC * NZ)
@@ -72,10 +73,14 @@
     load_neg.start()
 
     barrier = pltpu.get_barrier_semaphore()
-    partners = [other_core] + [at_x(1), at_x(NX - 1)]
-    partners += [at_y(step) for step in range(1, NY)] + [at_z(step) for step in range(1, NZ)]
+    partners = [at_y(step) for step in range(1, NY)] + [other_core, at_x(1), at_x(NX - 1)]
     for partner in partners:
         pl.semaphore_signal(barrier, inc=1, device_id=partner, device_id_type=MESH)
+
+    @pl.when(z != HUB)
+    def _():
+        pl.semaphore_signal(barrier, inc=1, device_id=((x * NZ + HUB) * NC + core, pa), device_id_type=MESH)
+
     rows[ROWS + BANK + SHARE:2 * ROWS, :] = jnp.zeros((ROWS - BANK - SHARE, D), BF16)
 
     lane = iota((ROWS, ROWS), 1)
@@ -106,14 +111,19 @@
     total_part[...] = jnp.broadcast_to(jnp.sum(exps_t, axis=0, keepdims=True), (8, ROWS))
     totals[pl.ds(pa, 1)] = total_part[...][None]
 
-    pl.semaphore_wait(barrier, len(partners))
-
-    for step in range(1, NY):
-        copy = pltpu.make_async_remote_copy(
+    pl.semaphore_wait(barrier, len(partners) + jnp.where(z == HUB, NZ - 1, 0))
+
+    @pl.when(z == HUB)
+    def _():
+        for step in range(1, NZ):
+            pl.semaphore_signal(all_here, inc=1, device_id=at_z(step), device_id_type=MESH)
+
+
+    for place in range(NY - 1):
+        pltpu.make_async_remote_copy(
             src_ref=total_part, dst_ref=totals.at[pa],
             send_sem=t_send_sem, recv_sem=t_recv_sem,
-            device_id=at_y(step), device_id_type=MESH)
-        copy.start()
+            device_id=(pb, place + jnp.where(place >= pa, 1, 0)), device_id_type=MESH).start()
 
     weight = jnp.transpose(exps_t * c_scale_col).astype(BF16)
 
@@ -169,12 +179,19 @@
             part[dest, cols] = part[dest, cols] + y_recv[s, m, j]
             y_send(s, m + 2, j)
 
+    order = jnp.where(sub < BANK, (sub % HALF_ROWS) * NC + sub // HALF_ROWS, sub)
+    move = jnp.where(lane == order, 1.0, 0.0).astype(BF16)
+    high = exps_t.astype(BF16)
+    rest = exps_t - high.astype(F32)
+    middle = rest.astype(BF16)
+    low = (rest - middle.astype(F32)).astype(BF16)
+    ordered = (jnp.dot(move, high, preferred_element_type=F32)
+               + jnp.dot(move, middle, preferred_element_type=F32)
+               + jnp.dot(move, low, preferred_element_type=F32))
+
     pltpu.make_async_copy(totals.at[1:NY], totals.at[1:NY], t_recv_sem).wait()
     total_row = jnp.sum(totals[...], axis=0)[0:1, :]
-    weight_t = (exps_t * (q_scale_row * INVERSE / total_row)).astype(BF16)
-    order = jnp.where(sub < BANK, (sub % HALF_ROWS) * NC + sub // HALF_ROWS, sub)
-    weight_t = jnp.dot(jnp.where(lane == order, 1.0, 0.0).astype(BF16), weight_t,
-                       preferred_element_type=F32).astype(BF16)
+    weight_t = (ordered * (q_scale_row * INVERSE / total_row)).astype(BF16)
 
     c_copies, x_copies = [], []
 
@@ -222,11 +239,9 @@
             own = core_rows(core)
             bank[piece, own, :] = bank[piece, own, :] + c_recv[piece]
 
-    def x_first(batch):
+    def x_first(batch, stage):
         for s in range(2):
-            x_send(1, 2 * batch + s, s)
-        for s in range(2):
-            x_send(2, 2 * batch + 1 - s, s)
+            x_send(stage, 2 * batch + (s if stage == 1 else 1 - s), s)
 
     def x1_step(batch):
         for s in range(2):
@@ -244,11 +259,12 @@
                 x_copy(2, piece, t).wait_recv()
             total = bank[piece, x_rows(0), :] + x_recv2[piece, 0] + x_recv2[piece, 1]
             z_send[batch, :, s * SUB:(s + 1) * SUB, :] = total.reshape(CHUNK, SUB, 128)
-        for step in range(1, NZ):
+        for place in range(NZ - 1):
+            target = place + jnp.where(place >= z, 1, 0)
             pltpu.make_async_remote_copy(
-                src_ref=z_send.at[batch, (z + step) % NZ], dst_ref=z_recv.at[batch, z],
+                src_ref=z_send.at[batch, target], dst_ref=z_recv.at[batch, z],
                 send_sem=z_send_sem.at[batch], recv_sem=z_recv_sem.at[batch],
-                device_id=at_z(step), device_id_type=MESH).start()
+                device_id=((x * NZ + target) * NC + core, pa), device_id_type=MESH).start()
         z_recv[batch, pl.ds(z, 1)] = z_send[batch, pl.ds(z, 1)]
 
     def z_step(batch):
@@ -266,18 +282,22 @@
     total_own = pick(own_query, total_row, 1)
     p_scale_own = pick(own_lane == own_sub + BANK, c_scale_row, 1)
 
-    c_step(0)
-    x_first(0)
-    c_step(1)
-    x_first(1)
+    for batch in range(NB):
+        c_step(batch)
+        x_first(batch, 1)
+        if batch < 2:
+            x_first(batch, 2)
     y_step(0, 0)
-    c_step(2)
-    c_step(3)
     x1_step(0)
-    x_first(2)
+    x_first(2, 2)
     y_step(0, 1)
     x1_step(1)
-    x_first(3)
+    x_first(3, 2)
+
+    @pl.when(z != HUB)
+    def _():
+        pl.semaphore_wait(all_here, 1)
+
     x2_step(0)
     y_step(1, 0)
     x1_step(2)
@@ -397,7 +417,7 @@
             dma((2, 4)), dma((4,)), dma, dma,
             dma((2, 7, 2)), dma((2, 7, 2)),
             dma((NT,)), dma((NT,)), dma((NT,)), dma((NT,)),
-            dma((NT, 2)), dma((NT, 2)), dma((NB,)), dma((NB,)),
+            dma((NT, 2)), dma((NT, 2)), dma((NB,)), dma((NB,)), pltpu.SemaphoreType.REGULAR,
         ],
         compiler_params=pltpu.CompilerParams(
             collective_id=0, has_side_effects=True, vmem_limit_bytes=40 * 1024 * 1024),

time: 48.4 us -> 42.8 us (0.88)
  the two profiles are of different devices: /device:TPU:8 before, /device:TPU:1 now
where the time goes in v3:
time: 42.8 us; the launch traced here: 42.2 us
  Pallas kernels  41.5 us (97%)
  between operations  0.64 us (1%)
    pallas_call x1, Pallas kernels, on_device(): pl.pallas_call(kernel, out_shape=(jax.ShapeDtypeStruct((SHARE, D), F32),...  40.7 us

profile of v3, /device:TPU:1, one launch (start us, length us, event | category | flops | bytes accessed | tf_op | source)
XLA Modules:
  0.0 42.2 jit_solution(8441424646707645594)
XLA Ops:
  0.6 40.7 %shard_map.75 = (f32[16,4096]{1,0:T(8,128)S(1)}, f32[16,4096]{1,0:T(8,128)S(1)}, f32[32,128]{1,0:T(8,128)S(1)}, f32[1,16]{1,0:T(1,128)S(1)}) custom-call(bf16[128,4096]{1,0:T(8,128)(2,1)} %q_hbm.1, bf16[16,4096]{1,0:T(8,128)(2,1)} %p_hbm.1, bf16[96,4096]{1,0:T(8,128)(2,1)} %b_hbm.1, s32[7,128]{1,0:T(8,128)} %bitcast.3), custom_call_target="tpu_custom_call" | custom-call | tf_op jit(solution)/shard_map/pallas_call | solution.py:388
  41.3 0.8 %shard_map.76 = (f32[16,4096]{1,0:T(8,128)}, f32[16,4096]{1,0:T(8,128)}, f32[32,128]{1,0:T(8,128)}, f32[1,16]{1,0:T(1,128)}) custom-call(f32[16,4096]{1,0:T(8,128)S(1)} %get-tuple-element.12.refs_0_, f32[16,4096]{1,0:T(8,128)S(1)} %get-tuple-element.13.refs_1_, f32[32,128]{1,0:T(8,128)S(1)} %get-tuple-element.14.refs_2_, f32[1,16]{1,0:T(1,128)S(1)} %get-tuple-element.15.refs_3_), custom_call_target="tpu_custom_call" | custom-call | tf_op jit(solution)/shard_map/pallas_call | solution.py:425

commit v4 on v3

--- a/solution.py
+++ b/solution.py
@@ -16,7 +16,7 @@
 SHARE = 16
 BANK = 96
 NEG = 7
-PIECE = 1024
+HALF = D // 2
 THIN = 512
 NT = D // THIN
 HUB = 9
@@ -43,7 +43,7 @@
     rows, neg, part, own_row, passage_up, out_q, out_p, out_b, out_loss,
     totals, total_part, y_recv, bank, c_recv, x_recv1, x_recv2, z_send, z_recv,
     load_sem, store_sem, t_send_sem, t_recv_sem, y_send_sem, y_recv_sem,
-    c_send_sem, c_recv_sem, x1_send_sem, x1_recv_sem, x2_send_sem, x2_recv_sem,
+    c_send_sem, c_recv_sem, x_send_sem, x1_recv_sem, x2_recv_sem,
     z_send_sem, z_recv_sem, all_here,
 ):
     pb, pa = lax.axis_index("pb"), lax.axis_index("pa")
@@ -60,17 +60,14 @@
 
     other_core = ((x * NZ + z) * NC + (1 - core), pa)
 
-    loads = []
-    for half in range(2):
-        cols = slice(half * (D // 2), (half + 1) * (D // 2))
-        for i, (source, first, count) in enumerate(
-                ((q_hbm, 0, ROWS), (b_hbm, ROWS, BANK), (p_hbm, ROWS + BANK, SHARE))):
-            loads.append(pltpu.make_async_copy(
-                source.at[:, cols], rows.at[first:first + count, cols], load_sem.at[half, i]))
-    load_neg = pltpu.make_async_copy(neg_hbm, neg, load_sem.at[0, 3])
+    loads = [
+        pltpu.make_async_copy(q_hbm, rows.at[0:ROWS], load_sem.at[0]),
+        pltpu.make_async_copy(b_hbm, rows.at[ROWS:ROWS + BANK], load_sem.at[0]),
+        pltpu.make_async_copy(p_hbm, rows.at[ROWS + BANK:ROWS + BANK + SHARE], load_sem.at[0]),
+        pltpu.make_async_copy(neg_hbm, neg, load_sem.at[1]),
+    ]
     for load in loads:
         load.start()
-    load_neg.start()
 
     barrier = pltpu.get_barrier_semaphore()
     partners = [at_y(step) for step in range(1, NY)] + [other_core, at_x(1), at_x(NX - 1)]
@@ -83,6 +80,9 @@
 
     rows[ROWS + BANK + SHARE:2 * ROWS, :] = jnp.zeros((ROWS - BANK - SHARE, D), BF16)
 
+    def arrive(like, sem):
+        pltpu.make_async_copy(like, like, sem).wait()
+
     lane = iota((ROWS, ROWS), 1)
     sub = iota((ROWS, ROWS), 0)
     eye = lane == sub
@@ -90,15 +90,10 @@
     def pick(mask, values, axis):
         return jnp.sum(jnp.where(mask, values, 0.0), axis=axis, keepdims=True)
 
-    gram_left, gram_c = 0.0, 0.0
-    for half in range(2):
-        for load in loads[3 * half:3 * half + 3]:
-            load.wait()
-        cols = slice(half * (D // 2), (half + 1) * (D // 2))
-        gram_left = gram_left + nt(rows[:, cols], rows[:ROWS, cols])
-        gram_c = gram_c + nt(rows[ROWS:, cols], rows[ROWS:, cols])
-    gram_q, raw = gram_left[:ROWS], gram_left[ROWS:]
-    load_neg.wait()
+    arrive(rows.at[0:ROWS + BANK + SHARE], load_sem.at[0])
+    gram = nt(rows[...], rows[...])
+    gram_q, raw, gram_c = gram[:ROWS, :ROWS], gram[ROWS:, :ROWS], gram[ROWS:, ROWS:]
+    loads[3].wait()
     q_scale_row = lax.rsqrt(pick(eye, gram_q, 0) + EPSILON)
     c_scale_col = lax.rsqrt(pick(eye, gram_c, 1) + EPSILON)
     c_scale_row = lax.rsqrt(pick(eye, gram_c, 0) + EPSILON)
@@ -127,9 +122,9 @@
 
     weight = jnp.transpose(exps_t * c_scale_col).astype(BF16)
 
-    def part_piece(piece):
-        for block in range(PIECE // 256):
-            cols = pl.ds(piece * PIECE + block * 256, 256)
+    def part_half(half):
+        for block in range(HALF // 256):
+            cols = pl.ds(half * HALF + block * 256, 256)
             part[:, cols] = jnp.dot(weight, rows[ROWS:, cols], preferred_element_type=F32)
 
     def y_rows(step):
@@ -138,46 +133,31 @@
     def y_distance(m):
         return 4 - (m + 1) // 2
 
-    def y_pieces(s, m):
-        half = s if m % 2 == 0 else 1 - s
-        return (2 * half, 2 * half + 1)
-
-    y_copies = []
-
-    def y_copy(s, m, j):
+    def y_half(s, m):
+        return s if m % 2 == 0 else 1 - s
+
+    def y_copy(s, m):
         sign = 1 if s == 0 else -1
-        piece = y_pieces(s, m)[j]
         return pltpu.make_async_remote_copy(
-            src_ref=part.at[y_rows((sign * y_distance(m)) % NY), pl.ds(piece * PIECE, PIECE)],
-            dst_ref=y_recv.at[s, m, j],
-            send_sem=y_send_sem.at[s, m, j], recv_sem=y_recv_sem.at[s, m, j],
+            src_ref=part.at[y_rows((sign * y_distance(m)) % NY), pl.ds(y_half(s, m) * HALF, HALF)],
+            dst_ref=y_recv.at[s, m],
+            send_sem=y_send_sem, recv_sem=y_recv_sem.at[s, m],
             device_id=at_y(sign % NY), device_id_type=MESH)
 
-    def y_send(s, m, j):
-        copy = y_copy(s, m, j)
-        copy.start()
-        y_copies.append(copy)
-
-    part_piece(0)
-    y_send(0, 0, 0)
-    part_piece(2)
-    y_send(1, 0, 0)
-    part_piece(1)
-    y_send(0, 0, 1)
-    part_piece(3)
-    y_send(1, 0, 1)
-    for j in range(2):
+    for s in range(2):
+        part_half(s)
+        y_copy(s, 0).start()
+    for s in range(2):
+        y_copy(s, 1).start()
+
+    def y_step(m):
         for s in range(2):
-            y_send(s, 1, j)
-
-    def y_step(m, j):
-        for s in range(2):
-            y_copy(s, m, j).wait_recv()
+            y_copy(s, m).wait_recv()
             sign = 1 if s == 0 else -1
             dest = y_rows((sign * (y_distance(m) - 1)) % NY)
-            cols = pl.ds(y_pieces(s, m)[j] * PIECE, PIECE)
-            part[dest, cols] = part[dest, cols] + y_recv[s, m, j]
-            y_send(s, m + 2, j)
+            cols = pl.ds(y_half(s, m) * HALF, HALF)
+            part[dest, cols] = part[dest, cols] + y_recv[s, m]
+            y_copy(s, m + 2).start()
 
     order = jnp.where(sub < BANK, (sub % HALF_ROWS) * NC + sub // HALF_ROWS, sub)
     move = jnp.where(lane == order, 1.0, 0.0).astype(BF16)
@@ -189,11 +169,9 @@
                + jnp.dot(move, middle, preferred_element_type=F32)
                + jnp.dot(move, low, preferred_element_type=F32))
 
-    pltpu.make_async_copy(totals.at[1:NY], totals.at[1:NY], t_recv_sem).wait()
+    arrive(totals.at[1:NY], t_recv_sem)
     total_row = jnp.sum(totals[...], axis=0)[0:1, :]
     weight_t = (ordered * (q_scale_row * INVERSE / total_row)).astype(BF16)
-
-    c_copies, x_copies = [], []
 
     def core_rows(which):
         return pl.ds(pl.multiple_of(which * (HALF_ROWS * SUB), HALF_ROWS * SUB), HALF_ROWS * SUB)
@@ -207,36 +185,28 @@
                 for c in range(2):
                     bank[piece, pl.ds(r * 8 * SUB + block * 2 + c, 8, stride=SUB), :] = (
                         product[r * 8:r * 8 + 8, c * 128:c * 128 + 128])
-        copy = pltpu.make_async_remote_copy(
+        pltpu.make_async_remote_copy(
             src_ref=bank.at[piece, core_rows(1 - core)], dst_ref=c_recv.at[piece],
-            send_sem=c_send_sem.at[piece], recv_sem=c_recv_sem.at[piece],
-            device_id=other_core, device_id_type=MESH)
-        copy.start()
-        c_copies.append(copy)
+            send_sem=c_send_sem, recv_sem=c_recv_sem.at[piece // 2],
+            device_id=other_core, device_id_type=MESH).start()
 
     def x_rows(step):
         start = core * (HALF_ROWS * SUB) + ((x + step) % NX) * (CHUNK * SUB)
         return pl.ds(pl.multiple_of(start, CHUNK * SUB), CHUNK * SUB)
 
-    def x_copy(stage, piece, s):
+    def x_send(stage, piece, s):
         sign = 1 if s == 0 else -1
-        recv = x_recv1.at[piece] if stage == 1 else x_recv2.at[piece, s]
-        send_sem = x1_send_sem.at[piece] if stage == 1 else x2_send_sem.at[piece, s]
-        recv_sem = x1_recv_sem.at[piece] if stage == 1 else x2_recv_sem.at[piece, s]
-        return pltpu.make_async_remote_copy(
-            src_ref=bank.at[piece, x_rows(2 if stage == 1 else sign % NX)], dst_ref=recv,
-            send_sem=send_sem, recv_sem=recv_sem,
-            device_id=at_x(sign % NX), device_id_type=MESH)
-
-    def x_send(stage, piece, s):
-        copy = x_copy(stage, piece, s)
-        copy.start()
-        x_copies.append(copy)
+        recv_sem = x1_recv_sem if stage == 1 else x2_recv_sem
+        pltpu.make_async_remote_copy(
+            src_ref=bank.at[piece, x_rows(2 if stage == 1 else sign % NX)],
+            dst_ref=x_recv1.at[piece] if stage == 1 else x_recv2.at[piece, s],
+            send_sem=x_send_sem.at[stage - 1], recv_sem=recv_sem.at[piece // 2],
+            device_id=at_x(sign % NX), device_id_type=MESH).start()
 
     def c_step(batch):
+        arrive(c_recv.at[2 * batch:2 * batch + 2], c_recv_sem.at[batch])
+        own = core_rows(core)
         for piece in (2 * batch, 2 * batch + 1):
-            c_copies[piece].wait_recv()
-            own = core_rows(core)
             bank[piece, own, :] = bank[piece, own, :] + c_recv[piece]
 
     def x_first(batch, stage):
@@ -244,33 +214,26 @@
             x_send(stage, 2 * batch + (s if stage == 1 else 1 - s), s)
 
     def x1_step(batch):
+        arrive(x_recv1.at[2 * batch:2 * batch + 2], x1_recv_sem.at[batch])
         for s in range(2):
             piece = 2 * batch + s
-            sign = 1 if s == 0 else -1
-            x_copy(1, piece, s).wait_recv()
-            dest = x_rows(sign % NX)
+            dest = x_rows((1 if s == 0 else -1) % NX)
             bank[piece, dest, :] = bank[piece, dest, :] + x_recv1[piece]
             x_send(2, piece, s)
 
     def x2_step(batch):
+        arrive(x_recv2.at[2 * batch:2 * batch + 2], x2_recv_sem.at[batch])
         for s in range(2):
             piece = 2 * batch + s
-            for t in range(2):
-                x_copy(2, piece, t).wait_recv()
             total = bank[piece, x_rows(0), :] + x_recv2[piece, 0] + x_recv2[piece, 1]
             z_send[batch, :, s * SUB:(s + 1) * SUB, :] = total.reshape(CHUNK, SUB, 128)
         for place in range(NZ - 1):
             target = place + jnp.where(place >= z, 1, 0)
             pltpu.make_async_remote_copy(
                 src_ref=z_send.at[batch, target], dst_ref=z_recv.at[batch, z],
-                send_sem=z_send_sem.at[batch], recv_sem=z_recv_sem.at[batch],
+                send_sem=z_send_sem, recv_sem=z_recv_sem,
                 device_id=((x * NZ + target) * NC + core, pa), device_id_type=MESH).start()
         z_recv[batch, pl.ds(z, 1)] = z_send[batch, pl.ds(z, 1)]
-
-    def z_step(batch):
-        rest = z_recv.at[batch, 1:NZ]
-        pltpu.make_async_copy(rest, rest, z_recv_sem.at[batch]).wait()
-        return jnp.sum(z_recv[batch], axis=0)
 
     def norm_back(wide, scale, upstream):
         inner = jnp.sum(wide * upstream, axis=1, keepdims=True)
@@ -285,28 +248,21 @@
     for batch in range(NB):
         c_step(batch)
         x_first(batch, 1)
-        if batch < 2:
-            x_first(batch, 2)
-    y_step(0, 0)
-    x1_step(0)
-    x_first(2, 2)
-    y_step(0, 1)
-    x1_step(1)
-    x_first(3, 2)
+    arrive(x_recv1, x_send_sem.at[0])
+    for batch in range(NB):
+        x_first(batch, 2)
+    for batch in range(NB):
+        x1_step(batch)
+    y_step(0)
 
     @pl.when(z != HUB)
     def _():
         pl.semaphore_wait(all_here, 1)
 
-    x2_step(0)
-    y_step(1, 0)
-    x1_step(2)
-    x2_step(1)
-    y_step(1, 1)
-    x1_step(3)
-    x2_step(2)
-    y_step(2, 0)
-    x2_step(3)
+    for batch in range(NB):
+        x2_step(batch)
+        if batch == 1:
+            y_step(1)
 
     own_q_rows = pl.ds(pl.multiple_of(pa * SHARE, SHARE), SHARE)
     own_q = rows[own_q_rows, :].astype(F32)
@@ -321,7 +277,7 @@
     store_loss = pltpu.make_async_copy(out_loss, loss_hbm, store_sem.at[1])
     store_loss.start()
 
-    y_step(2, 1)
+    y_step(2)
 
     one_hot = jnp.where(iota((SHARE, ROWS), 1) == pb, 1.0, 0.0).astype(BF16)
     for block in range(D // 256):
@@ -329,26 +285,22 @@
         for c in range(2):
             own_row[block * 2 + c:block * 2 + c + 1, :] = row[0:1, c * 128:c * 128 + 128]
 
-    y_step(3, 0)
-    y_step(3, 1)
-    y_step(4, 0)
-    y_step(4, 1)
+    y_step(3)
+    y_step(4)
 
     inverse_own = INVERSE / total_own
     own = y_rows(0)
     inner = jnp.zeros((SHARE, 1), F32)
     for m in (5, 6):
-        for j in range(2):
-            for s in range(2):
-                y_copy(s, m, j).wait_recv()
-    for piece in range(D // PIECE):
-        half, j = piece // 2, piece % 2
-        cols = pl.ds(piece * PIECE, PIECE)
-        arrived = y_recv[0, 6 if half == 0 else 5, j] + y_recv[1, 5 if half == 0 else 6, j]
+        for s in range(2):
+            y_copy(s, m).wait_recv()
+    for half in range(2):
+        cols = slice(half * HALF, (half + 1) * HALF)
+        arrived = y_recv[0, 6 if half == 0 else 5] + y_recv[1, 5 if half == 0 else 6]
         value = (part[own, cols] + arrived) * inverse_own
-        value = value - own_p[:, piece * PIECE:(piece + 1) * PIECE] * (p_scale_own * INVERSE)
+        value = value - own_p[:, cols] * (p_scale_own * INVERSE)
         out_q[:, cols] = value
-        inner = inner + jnp.sum(value * own_q[:, piece * PIECE:(piece + 1) * PIECE], axis=1, keepdims=True)
+        inner = inner + jnp.sum(value * own_q[:, cols], axis=1, keepdims=True)
     out_q[...] = q_scale_own * out_q[...] - (q_scale_own * q_scale_own * q_scale_own * inner) * own_q
     store_q = pltpu.make_async_copy(out_q, qg_hbm, store_sem.at[3])
     store_q.start()
@@ -358,16 +310,16 @@
 
     wide = own_row[...]
     scale = lax.rsqrt(whole(wide * wide) + EPSILON)
-    for copy in y_copies + c_copies + x_copies:
-        copy.wait_send()
-    pltpu.make_async_copy(totals.at[1:NY], totals.at[1:NY], t_send_sem).wait()
-    for batch in range(NB):
-        rest = z_send.at[batch, 1:NZ]
-        pltpu.make_async_copy(rest, rest, z_send_sem.at[batch]).wait()
+    arrive(totals.at[1:NY], t_send_sem)
+    arrive(y_recv, y_send_sem)
+    arrive(c_recv, c_send_sem)
+    arrive(x_recv2, x_send_sem.at[1])
+    arrive(z_send.at[:, 1:NZ], z_send_sem)
     for store in (store_p, store_loss, store_q):
         store.wait()
 
-    bank_v = jnp.concatenate([z_step(batch) for batch in range(NB)], axis=0)
+    arrive(z_recv.at[:, 1:NZ], z_recv_sem)
+    bank_v = jnp.sum(z_recv[...], axis=1).reshape(D // 128, 128)
     out_b[...] = scale * bank_v - (scale * scale * scale * whole(wide * bank_v)) * wide
     store_b = pltpu.make_async_copy(out_b, bg_hbm, store_sem.at[2])
     store_b.start()
@@ -407,17 +359,16 @@
             pltpu.VMEM((1, SHARE), F32),
             pltpu.VMEM((NY, 8, ROWS), F32),
             pltpu.VMEM((8, ROWS), F32),
-            pltpu.VMEM((2, 7, 2, SHARE, PIECE), F32),
+            pltpu.VMEM((2, 7, SHARE, HALF), F32),
             pltpu.VMEM((NT, BANK * SUB, 128), F32),
             pltpu.VMEM((NT, HALF_ROWS * SUB, 128), F32),
             pltpu.VMEM((NT, CHUNK * SUB, 128), F32),
             pltpu.VMEM((NT, 2, CHUNK * SUB, 128), F32),
             pltpu.VMEM((NB, CHUNK, 2 * SUB, 128), F32),
             pltpu.VMEM((NB, CHUNK, 2 * SUB, 128), F32),
-            dma((2, 4)), dma((4,)), dma, dma,
-            dma((2, 7, 2)), dma((2, 7, 2)),
-            dma((NT,)), dma((NT,)), dma((NT,)), dma((NT,)),
-            dma((NT, 2)), dma((NT, 2)), dma((NB,)), dma((NB,)), pltpu.SemaphoreType.REGULAR,
+            dma((2,)), dma((4,)), dma, dma, dma, dma((2, 7)),
+            dma, dma((NB,)), dma((2,)), dma((NB,)), dma((NB,)),
+            dma, dma, pltpu.SemaphoreType.REGULAR,
         ],
         compiler_params=pltpu.CompilerParams(
             collective_id=0, has_side_effects=True, vmem_limit_bytes=40 * 1024 * 1024),

time: 42.8 us -> 41.5 us (0.970)
  Pallas kernels: 41.5 us -> 40.1 us
    pallas_call x1, Pallas kernels: 40.7 us -> 39.3 us  [on_device(): pl.pallas_call(kernel, out_shape=(jax.ShapeDtypeStruct((SHARE, D), F32),...]
where the time goes in v4:
time: 41.5 us; the launch traced here: 40.8 us
  Pallas kernels  40.1 us (97%)
  between operations  0.64 us (2%)
    pallas_call x1, Pallas kernels, on_device(): pl.pallas_call(kernel, out_shape=(jax.ShapeDtypeStruct((SHARE, D), F32),...  39.3 us
    pallas_call x1, Pallas kernels, on_device(): pl.pallas_call(hand_over, out_shape=(jax.ShapeDtypeStruct((SHARE, D), F32...  0.83 us

profile of v4, /device:TPU:1, one launch (start us, length us, event | category | flops | bytes accessed | tf_op | source)
XLA Modules:
  0.0 40.8 jit_solution(17129216593039165348)
XLA Ops:
  0.6 39.3 %shard_map.75 = (f32[16,4096]{1,0:T(8,128)S(1)}, f32[16,4096]{1,0:T(8,128)S(1)}, f32[32,128]{1,0:T(8,128)S(1)}, f32[1,16]{1,0:T(1,128)S(1)}) custom-call(bf16[128,4096]{1,0:T(8,128)(2,1)} %q_hbm.1, bf16[16,4096]{1,0:T(8,128)(2,1)} %p_hbm.1, bf16[96,4096]{1,0:T(8,128)(2,1)} %b_hbm.1, s32[7,128]{1,0:T(8,128)} %bitcast.3), custom_call_target="tpu_custom_call" | custom-call | tf_op jit(solution)/shard_map/pallas_call | solution.py:340
  39.9 0.8 %shard_map.76 = (f32[16,4096]{1,0:T(8,128)}, f32[16,4096]{1,0:T(8,128)}, f32[32,128]{1,0:T(8,128)}, f32[1,16]{1,0:T(1,128)}) custom-call(f32[16,4096]{1,0:T(8,128)S(1)} %get-tuple-element.12.refs_0_, f32[16,4096]{1,0:T(8,128)S(1)} %get-tuple-element.13.refs_1_, f32[32,128]{1,0:T(8,128)S(1)} %get-tuple-element.14.refs_2_, f32[1,16]{1,0:T(1,128)S(1)} %get-tuple-element.15.refs_3_), custom_call_target="tpu_custom_call" | custom-call | tf_op jit(solution)/shard_map/pallas_call | solution.py:376

commit v5 on v4

--- a/solution.py
+++ b/solution.py
@@ -17,13 +17,14 @@
 BANK = 96
 NEG = 7
 HALF = D // 2
-THIN = 512
-NT = D // THIN
+SUB = HALF // 128
 HUB = 9
-NB = NT // 2
-SUB = THIN // 128
-HALF_ROWS = BANK // NC
+NB = 4
+GROUP = NZ // NB
+BATCH_ROWS = BANK // NB
+HALF_ROWS = BATCH_ROWS // NC
 CHUNK = HALF_ROWS // NX
+NT = 2 * NB
 F32 = jnp.float32
 BF16 = jnp.bfloat16
 MESH = pl.DeviceIdType.MESH
@@ -159,7 +160,10 @@
             part[dest, cols] = part[dest, cols] + y_recv[s, m]
             y_copy(s, m + 2).start()
 
-    order = jnp.where(sub < BANK, (sub % HALF_ROWS) * NC + sub // HALF_ROWS, sub)
+    place = sub % BATCH_ROWS
+    place_core, place_x, place_z = place // HALF_ROWS, (place % HALF_ROWS) // CHUNK, place % CHUNK
+    bank_row = place_x * (NZ * NC) + ((sub // BATCH_ROWS) * GROUP + place_z) * NC + place_core
+    order = jnp.where(sub < BANK, bank_row, sub)
     move = jnp.where(lane == order, 1.0, 0.0).astype(BF16)
     high = exps_t.astype(BF16)
     rest = exps_t - high.astype(F32)
@@ -176,19 +180,25 @@
     def core_rows(which):
         return pl.ds(pl.multiple_of(which * (HALF_ROWS * SUB), HALF_ROWS * SUB), HALF_ROWS * SUB)
 
-    for piece in range(NT):
-        for block in range(THIN // 256):
-            cols = pl.ds(piece * THIN + block * 256, 256)
+    def c_copy(piece):
+        return pltpu.make_async_remote_copy(
+            src_ref=bank.at[piece, core_rows(1 - core)], dst_ref=c_recv.at[piece],
+            send_sem=c_send_sem, recv_sem=c_recv_sem.at[piece // 2],
+            device_id=other_core, device_id_type=MESH)
+
+    for half in range(2):
+        for block in range(HALF // 256):
+            cols = pl.ds(half * HALF + block * 256, 256)
             product = jnp.dot(weight_t, rows[0:ROWS, cols], preferred_element_type=F32)
             passage_up[:, cols] = product[BANK:BANK + SHARE, :]
             for r in range(BANK // 8):
+                batch, r8 = r // (BATCH_ROWS // 8), r % (BATCH_ROWS // 8)
                 for c in range(2):
-                    bank[piece, pl.ds(r * 8 * SUB + block * 2 + c, 8, stride=SUB), :] = (
+                    bank[2 * batch + half, pl.ds(r8 * 8 * SUB + block * 2 + c, 8, stride=SUB), :] = (
                         product[r * 8:r * 8 + 8, c * 128:c * 128 + 128])
-        pltpu.make_async_remote_copy(
-            src_ref=bank.at[piece, core_rows(1 - core)], dst_ref=c_recv.at[piece],
-            send_sem=c_send_sem, recv_sem=c_recv_sem.at[piece // 2],
-            device_id=other_core, device_id_type=MESH).start()
+        c_copy(half).start()
+    for piece in range(2, NT):
+        c_copy(piece).start()
 
     def x_rows(step):
         start = core * (HALF_ROWS * SUB) + ((x + step) % NX) * (CHUNK * SUB)
@@ -226,14 +236,14 @@
         for s in range(2):
             piece = 2 * batch + s
             total = bank[piece, x_rows(0), :] + x_recv2[piece, 0] + x_recv2[piece, 1]
-            z_send[batch, :, s * SUB:(s + 1) * SUB, :] = total.reshape(CHUNK, SUB, 128)
-        for place in range(NZ - 1):
-            target = place + jnp.where(place >= z, 1, 0)
-            pltpu.make_async_remote_copy(
-                src_ref=z_send.at[batch, target], dst_ref=z_recv.at[batch, z],
-                send_sem=z_send_sem, recv_sem=z_recv_sem,
-                device_id=((x * NZ + target) * NC + core, pa), device_id_type=MESH).start()
-        z_recv[batch, pl.ds(z, 1)] = z_send[batch, pl.ds(z, 1)]
+            z_send[batch * GROUP:(batch + 1) * GROUP, s * SUB:(s + 1) * SUB, :] = total.reshape(CHUNK, SUB, 128)
+        for target in range(batch * GROUP, (batch + 1) * GROUP):
+            @pl.when(z != target)
+            def _():
+                pltpu.make_async_remote_copy(
+                    src_ref=z_send.at[target], dst_ref=z_recv.at[z],
+                    send_sem=z_send_sem, recv_sem=z_recv_sem,
+                    device_id=((x * NZ + target) * NC + core, pa), device_id_type=MESH).start()
 
     def norm_back(wide, scale, upstream):
         inner = jnp.sum(wide * upstream, axis=1, keepdims=True)
@@ -245,24 +255,36 @@
     total_own = pick(own_query, total_row, 1)
     p_scale_own = pick(own_lane == own_sub + BANK, c_scale_row, 1)
 
-    for batch in range(NB):
-        c_step(batch)
-        x_first(batch, 1)
-    arrive(x_recv1, x_send_sem.at[0])
-    for batch in range(NB):
-        x_first(batch, 2)
-    for batch in range(NB):
-        x1_step(batch)
+    c_step(0)
+    x_first(0, 1)
+    x_first(0, 2)
     y_step(0)
+    c_step(1)
+    c_step(2)
+    c_step(3)
+    x1_step(0)
+    x_first(1, 1)
+    x_first(1, 2)
+    x_first(2, 1)
+    y_step(1)
 
     @pl.when(z != HUB)
     def _():
         pl.semaphore_wait(all_here, 1)
 
-    for batch in range(NB):
-        x2_step(batch)
-        if batch == 1:
-            y_step(1)
+    x2_step(0)
+    x1_step(1)
+    x_first(2, 2)
+    x_first(3, 1)
+    y_step(2)
+    x1_step(2)
+    x_first(3, 2)
+    x2_step(1)
+    x1_step(3)
+    y_step(3)
+    x2_step(2)
+    x2_step(3)
+    z_recv[pl.ds(z, 1)] = z_send[pl.ds(z, 1)]
 
     own_q_rows = pl.ds(pl.multiple_of(pa * SHARE, SHARE), SHARE)
     own_q = rows[own_q_rows, :].astype(F32)
@@ -277,7 +299,8 @@
     store_loss = pltpu.make_async_copy(out_loss, loss_hbm, store_sem.at[1])
     store_loss.start()
 
-    y_step(2)
+
+    y_step(4)
 
     one_hot = jnp.where(iota((SHARE, ROWS), 1) == pb, 1.0, 0.0).astype(BF16)
     for block in range(D // 256):
@@ -285,8 +308,6 @@
         for c in range(2):
             own_row[block * 2 + c:block * 2 + c + 1, :] = row[0:1, c * 128:c * 128 + 128]
 
-    y_step(3)
-    y_step(4)
 
     inverse_own = INVERSE / total_own
     own = y_rows(0)
@@ -314,12 +335,13 @@
     arrive(y_recv, y_send_sem)
     arrive(c_recv, c_send_sem)
     arrive(x_recv2, x_send_sem.at[1])
-    arrive(z_send.at[:, 1:NZ], z_send_sem)
+    arrive(z_send.at[1:NZ], z_send_sem)
+    arrive(x_recv1, x_send_sem.at[0])
     for store in (store_p, store_loss, store_q):
         store.wait()
 
-    arrive(z_recv.at[:, 1:NZ], z_recv_sem)
-    bank_v = jnp.sum(z_recv[...], axis=1).reshape(D // 128, 128)
+    arrive(z_recv.at[1:NZ], z_recv_sem)
+    bank_v = jnp.sum(z_recv[...], axis=0)
     out_b[...] = scale * bank_v - (scale * scale * scale * whole(wide * bank_v)) * wide
     store_b = pltpu.make_async_copy(out_b, bg_hbm, store_sem.at[2])
     store_b.start()
@@ -360,12 +382,12 @@
             pltpu.VMEM((NY, 8, ROWS), F32),
             pltpu.VMEM((8, ROWS), F32),
             pltpu.VMEM((2, 7, SHARE, HALF), F32),
-            pltpu.VMEM((NT, BANK * SUB, 128), F32),
+            pltpu.VMEM((NT, BATCH_ROWS * SUB, 128), F32),
             pltpu.VMEM((NT, HALF_ROWS * SUB, 128), F32),
             pltpu.VMEM((NT, CHUNK * SUB, 128), F32),
             pltpu.VMEM((NT, 2, CHUNK * SUB, 128), F32),
-            pltpu.VMEM((NB, CHUNK, 2 * SUB, 128), F32),
-            pltpu.VMEM((NB, CHUNK, 2 * SUB, 128), F32),
+            pltpu.VMEM((NZ, D // 128, 128), F32),
+            pltpu.VMEM((NZ, D // 128, 128), F32),
             dma((2,)), dma((4,)), dma, dma, dma, dma((2, 7)),
             dma, dma((NB,)), dma((2,)), dma((NB,)), dma((NB,)),
             dma, dma, pltpu.SemaphoreType.REGULAR,

time: 41.5 us -> 40.5 us (0.976); the launches traced: 40.8 us -> 40.4 us
  no operation moved by 1% of the time
where the time goes in v5:
time: 40.5 us; the launch traced here: 40.4 us
  Pallas kernels  39.7 us (98%)
  between operations  0.64 us (2%)
    pallas_call x1, Pallas kernels, on_device(): pl.pallas_call(kernel, out_shape=(jax.ShapeDtypeStruct((SHARE, D), F32),...  38.9 us
    pallas_call x1, Pallas kernels, on_device(): pl.pallas_call(hand_over, out_shape=(jax.ShapeDtypeStruct((SHARE, D), F32...  0.83 us

profile of v5, /device:TPU:1, one launch (start us, length us, event | category | flops | bytes accessed | tf_op | source)
XLA Modules:
  0.0 40.4 jit_solution(2257338932830489257)
XLA Ops:
  0.6 38.9 %shard_map.75 = (f32[16,4096]{1,0:T(8,128)S(1)}, f32[16,4096]{1,0:T(8,128)S(1)}, f32[32,128]{1,0:T(8,128)S(1)}, f32[1,16]{1,0:T(1,128)S(1)}) custom-call(bf16[128,4096]{1,0:T(8,128)(2,1)} %q_hbm.1, bf16[16,4096]{1,0:T(8,128)(2,1)} %p_hbm.1, bf16[96,4096]{1,0:T(8,128)(2,1)} %b_hbm.1, s32[7,128]{1,0:T(8,128)} %bitcast.3), custom_call_target="tpu_custom_call" | custom-call | tf_op jit(solution)/shard_map/pallas_call | solution.py:362
  39.5 0.8 %shard_map.76 = (f32[16,4096]{1,0:T(8,128)}, f32[16,4096]{1,0:T(8,128)}, f32[32,128]{1,0:T(8,128)}, f32[1,16]{1,0:T(1,128)}) custom-call(f32[16,4096]{1,0:T(8,128)S(1)} %get-tuple-element.12.refs_0_, f32[16,4096]{1,0:T(8,128)S(1)} %get-tuple-element.13.refs_1_, f32[32,128]{1,0:T(8,128)S(1)} %get-tuple-element.14.refs_2_, f32[1,16]{1,0:T(1,128)S(1)} %get-tuple-element.15.refs_3_), custom_call_target="tpu_custom_call" | custom-call | tf_op jit(solution)/shard_map/pallas_call | solution.py:398

commit v6 on v5

--- a/solution.py
+++ b/solution.py
@@ -273,15 +273,15 @@
         pl.semaphore_wait(all_here, 1)
 
     x2_step(0)
+    y_step(2)
     x1_step(1)
     x_first(2, 2)
     x_first(3, 1)
-    y_step(2)
+    x2_step(1)
     x1_step(2)
     x_first(3, 2)
-    x2_step(1)
+    y_step(3)
     x1_step(3)
-    y_step(3)
     x2_step(2)
     x2_step(3)
     z_recv[pl.ds(z, 1)] = z_send[pl.ds(z, 1)]

time: 40.5 us -> 40.6 us (level)
  no operation moved by 1% of the time
where the time goes in v6:
time: 40.6 us; the launch traced here: 40.4 us
  Pallas kernels  39.8 us (98%)
  between operations  0.64 us (2%)
    pallas_call x1, Pallas kernels, on_device(): pl.pallas_call(kernel, out_shape=(jax.ShapeDtypeStruct((SHARE, D), F32),...  38.9 us
    pallas_call x1, Pallas kernels, on_device(): pl.pallas_call(hand_over, out_shape=(jax.ShapeDtypeStruct((SHARE, D), F32...  0.83 us

profile of v6, /device:TPU:1, one launch (start us, length us, event | category | flops | bytes accessed | tf_op | source)
XLA Modules:
  0.0 40.4 jit_solution(12863243564891103744)
XLA Ops:
  0.6 38.9 %shard_map.75 = (f32[16,4096]{1,0:T(8,128)S(1)}, f32[16,4096]{1,0:T(8,128)S(1)}, f32[32,128]{1,0:T(8,128)S(1)}, f32[1,16]{1,0:T(1,128)S(1)}) custom-call(bf16[128,4096]{1,0:T(8,128)(2,1)} %q_hbm.1, bf16[16,4096]{1,0:T(8,128)(2,1)} %p_hbm.1, bf16[96,4096]{1,0:T(8,128)(2,1)} %b_hbm.1, s32[7,128]{1,0:T(8,128)} %bitcast.3), custom_call_target="tpu_custom_call" | custom-call | tf_op jit(solution)/shard_map/pallas_call | solution.py:362
  39.6 0.8 %shard_map.76 = (f32[16,4096]{1,0:T(8,128)}, f32[16,4096]{1,0:T(8,128)}, f32[32,128]{1,0:T(8,128)}, f32[1,16]{1,0:T(1,128)}) custom-call(f32[16,4096]{1,0:T(8,128)S(1)} %get-tuple-element.12.refs_0_, f32[16,4096]{1,0:T(8,128)S(1)} %get-tuple-element.13.refs_1_, f32[32,128]{1,0:T(8,128)S(1)} %get-tuple-element.14.refs_2_, f32[1,16]{1,0:T(1,128)S(1)} %get-tuple-element.15.refs_3_), custom_call_target="tpu_custom_call" | custom-call | tf_op jit(solution)/shard_map/pallas_call | solution.py:398
